TPU v7x, 768 devices: a whole 4x8x12 slice. The times are simulated.
768 devices in a mesh: dp: 96 (over x, z, core), expert: 8 (over y).
Axes of the slice: x: 4, y: 8, z: 12, core: 2. Of those that a mesh axis runs over, the one named last changes fastest.
Arguments:
- grad_out: bfloat16 [30720, 3840], P(('dp', 'expert')), may hold values from -2.5 to 2.5
- routing: int32 [30720, 8], P(('dp', 'expert')), may hold values from 0 to 15, as said below
- probs: bfloat16 [30720, 8], P(('dp', 'expert')), may hold values from 0.099609375 to 1
- down_weight: bfloat16 [3840, 2048], P('dp', 'expert'), may hold values from -0.1875 to 0.1875
- gate_saved: bfloat16 [768, 30, 2048], P('dp', None, 'expert'), may hold values from -6 to 6
- up_saved: bfloat16 [768, 30, 2048], P('dp', None, 'expert'), may hold values from -6 to 6
Outputs:
- down_grad: float32 [3840, 2048], P('dp', 'expert')
- gate_grad: bfloat16 [768, 30, 2048], P('dp', None, 'expert')
- up_grad: bfloat16 [768, 30, 2048], P('dp', None, 'expert')
- prob_grad: float32 [30720, 8], P(('dp', 'expert'))
Inputs may be any that keep to these rules, and one draw needn't show every extreme that they name: `routing`: each row names 8 different experts; among one device's 40 tokens at most 30 name any one expert below 2; in every draw on some index of dp all devices' tokens name one such expert exactly 30 times.
All inputs are finite; a program needn't handle non-finite values.
Results may differ from a plain program's by a relative error of at most 0.003.
Values may be sent and summed in bfloat16 or wider, within the bound.
A program may use at most 32 MiB of HBM per device.

v0:
```python
import jax
import jax.numpy as jnp
from jax import lax
from jax.sharding import PartitionSpec as P

FLIGHT = 2


def slot_tables(route, expert, slots):
    hit = route == expert
    onrow = jnp.any(hit, axis=-1)
    slot = jnp.cumsum(onrow.astype(jnp.int32), axis=-1) - 1
    table = (slot[..., None, :] == jnp.arange(slots, dtype=jnp.int32)[:, None]) & onrow[
        ..., None, :
    ]
    return (hit, table.astype(jnp.float32))


def body(grad_out, routing, probs, down_weight, gate_saved, up_saved):
    n_experts = lax.axis_size("expert")
    sharing = n_experts // FLIGHT
    slots = gate_saved.shape[1]
    hid_units = gate_saved.shape[2]
    width = grad_out.shape[1]
    held = jnp.arange(FLIGHT, dtype=jnp.int32)[:, None, None]
    hits, tables = slot_tables(routing[None], held, slots)
    weights_tok = jnp.sum(
        jnp.where(hits, probs[None].astype(jnp.float32), jnp.float32(0.0)), axis=-1
    )
    packed = jnp.einsum(
        "ect,td->ecd", tables.astype(jnp.bfloat16), grad_out, preferred_element_type=jnp.float32
    ).astype(jnp.bfloat16)
    slot_prob = jnp.einsum(
        "ect,et->ec", tables, weights_tok, precision=lax.Precision.HIGHEST
    ).astype(jnp.bfloat16)
    rows, row_prob = (
        lax.all_to_all(
            jnp.repeat(packed, sharing, axis=0), "expert", split_axis=0, concat_axis=0, tiled=True
        ),
        lax.all_to_all(
            jnp.repeat(slot_prob, sharing, axis=0),
            "expert",
            split_axis=0,
            concat_axis=0,
            tiled=True,
        ),
    )
    flat = rows.reshape(n_experts * slots, width)
    columns = flat
    dh = jnp.dot(
        columns,
        lax.all_gather(down_weight, "dp", axis=0, tiled=True),
        preferred_element_type=jnp.float32,
    )
    gate = gate_saved.reshape(-1, hid_units).astype(jnp.float32)
    upper = up_saved.reshape(-1, hid_units).astype(jnp.float32)
    sig = jax.nn.sigmoid(gate)
    act = gate * sig
    hidden = act * upper
    scale_col = row_prob.reshape(-1, 1).astype(jnp.float32)
    scaled = scale_col * dh
    up_grad = (scaled * act).astype(jnp.bfloat16).reshape(gate_saved.shape)
    gate_grad = (
        (scaled * upper * sig * (1.0 + gate * (1.0 - sig)))
        .astype(jnp.bfloat16)
        .reshape(gate_saved.shape)
    )
    weighted = (scale_col * hidden).astype(jnp.bfloat16)
    partial_val = jnp.sum(hidden * dh, axis=-1).reshape(n_experts, slots)
    columns = flat
    down_grad = lax.psum_scatter(
        lax.dot_general(
            columns, weighted, (((0,), (0,)), ((), ())), preferred_element_type=jnp.float32
        ),
        "dp",
        scatter_dimension=0,
        tiled=True,
    )
    returned = lax.all_to_all(partial_val, "expert", split_axis=0, concat_axis=0, tiled=True)
    per_expert = jnp.sum(returned.reshape(FLIGHT, sharing, slots), axis=1)
    tok_val = jnp.einsum("ect,ec->et", tables, per_expert, precision=lax.Precision.HIGHEST)
    prob_grad = jnp.sum(jnp.where(hits, tok_val[:, :, None], jnp.float32(0.0)), axis=0)
    return (down_grad, gate_grad, up_grad, prob_grad)


def solution(mesh):
    in_specs = (
        P(("dp", "expert"), None),
        P(("dp", "expert"), None),
        P(("dp", "expert"), None),
        P("dp", "expert"),
        P("dp", None, "expert"),
        P("dp", None, "expert"),
    )
    out_specs = (
        P("dp", "expert"),
        P("dp", None, "expert"),
        P("dp", None, "expert"),
        P(("dp", "expert"), None),
    )
    return jax.shard_map(body, mesh=mesh, in_specs=in_specs, out_specs=out_specs, check_vma=False)
```

profile of v0, /device:TPU:8, one launch (start us, length us, event | category | flops | bytes accessed | tf_op | source)
XLA Modules:
  0.0 378.4 jit_solution(9261037355991297166)
XLA Ops:
  7.2 0.0 copy-start
  7.2 0.0 all-gather.2.cloned.1.call-start
  7.2 0.7 all-gather.2.cloned.1.call-update
  7.9 0.7 fusion.14
  8.6 0.2 reduce_window_sum.11
  8.9 0.0 copy-done
  8.9 0.3 convolution_convert_fusion
  9.1 1.4 broadcast_in_dim.34
  10.6 0.0 copy-start.1
  10.6 0.0 copy-start.2
  10.6 13.1 %all-to-all-start = ((bf16[8,30,3840]{2,1,0:T(8,128)(2,1)}), bf16[8,30,3840]{2,1,0:T(8,128)(2,1)S(1)}, u32[]{:S(2)}, u32[]{:S(2)}) async-start(bf16[8,30,3840]{2,1,0:T(8,128)(2,1)} %bitcast.1), calls=%async_computation | async-start | bytes 3932160 | tf_op jit(solution)/shard_map/all_to_all | solution.py:37
  23.7 0.0 copy-done.1
  23.7 0.0 copy-done.2
  23.8 41.4 %all-to-all-done = bf16[8,30,3840]{2,1,0:T(8,128)(2,1)S(1)} async-done(((bf16[8,30,3840]{2,1,0:T(8,128)(2,1)}), bf16[8,30,3840]{2,1,0:T(8,128)(2,1)S(1)}, u32[]{:S(2)}, u32[]{:S(2)}) %all-to-all-start) | async-done | bytes 1843232 | tf_op jit(solution)/shard_map/all_to_all | solution.py:37
  65.2 1.5 reshape.73
  66.7 0.0 copy-start.4
  66.7 0.0 copy-start.3
  66.7 67.4 %all-gather.2.cloned.1.call-done = bf16[3840,256]{1,0:T(8,128)(2,1)} async-done(((bf16[40,256]{1,0:T(8,128)(2,1)}), bf16[3840,256]{1,0:T(8,128)(2,1)}) %all-gather.2.cloned.1.call-update) | async-done | bytes 1966096 | tf_op jit(solution)/shard_map/all_gather | solution.py:52
  134.1 2.8 multiply_reduce_fusion
  136.9 0.7 all_to_all.18
  137.6 7.3 %all-to-all-start.2 = ((f32[8,1,30]{2,1,0:T(1,128)}), f32[8,1,30]{2,1,0:T(1,128)S(1)}, u32[]{:S(2)}, u32[]{:S(2)}) async-start(f32[8,1,30]{2,1,0:T(1,128)} %all_to_all.18), calls=%async_computation.3 | async-start | bytes 8192 | tf_op jit(solution)/shard_map/all_to_all | solution.py:79
  144.9 0.0 reduce-scatter.2.cloned.1.call-start
  144.9 0.0 copy-done.4
  144.9 6.1 %all-to-all-done.2 = f32[8,1,30]{2,1,0:T(1,128)S(1)} async-done(((f32[8,1,30]{2,1,0:T(1,128)}), f32[8,1,30]{2,1,0:T(1,128)S(1)}, u32[]{:S(2)}, u32[]{:S(2)}) %all-to-all-start.2) | async-done | bytes 992 | tf_op jit(solution)/shard_map/all_to_all | solution.py:79
  151.1 0.1 fusion.4
  151.2 0.0 copy-done.3
  151.2 0.6 select_reduce_fusion
  151.8 0.1 fusion.6
  152.0 10.0 %all_to_all.23 = bf16[8,1,30]{2,1,0:T(2,128)(2,1)S(1)} all-to-all(bf16[8,1,30]{2,1,0:T(2,128)(2,1)S(1)} %copy.41), channel_id=1, replica_groups=mesh['dp'=96,'expert'=8] {'expert'}, dimensions={0} | all-to-all | bytes 960 | tf_op jit(solution)/shard_map/all_to_all | solution.py:40
  162.0 0.1 copy.42
  162.1 0.1 multiply_convert_fusion.2
  162.2 2.6 convolution_bitcast_fusion
  164.8 0.0 reduce-scatter.2.cloned.1.call-update
  164.9 0.1 reshape.78
  165.0 0.2 multiply_convert_fusion
  165.2 0.7 copy.46
  165.9 0.7 copy.47
  166.7 204.9 %reduce-scatter.2.cloned.1.call-done = f32[40,256]{1,0:T(8,128)} async-done(((f32[3840,256]{1,0:T(8,128)}), f32[40,256]{1,0:T(8,128)}) %reduce-scatter.2.cloned.1.call-update) | async-done | bytes 40976 | tf_op jit(solution)/shard_map/reduce_scatter | solution.py:71
  (15 shorter events, 0.3 us)
Async XLA Ops:
  7.2 1.7 copy-start
  7.2 126.9 %all-gather.2.cloned.1.call-start = ((), (), s32[]{:S(2)}) async-start(), calls=%async_computation.5 | async-start | bytes 1986560 | tf_op jit(solution)/shard_map/all_gather | solution.py:52
  10.6 13.1 %copy-start.1 = (bf16[8,30,256]{2,0,1:T(8,128)(2,1)S(1)}, bf16[8,30,256]{2,0,1:T(8,128)(2,1)}, u32[]{:S(2)}) copy-start(bf16[8,30,256]{2,0,1:T(8,128)(2,1)} %param.11) | copy-start | bytes 368644
  10.6 13.2 %copy-start.2 = (bf16[8,30,256]{2,0,1:T(8,128)(2,1)S(1)}, bf16[8,30,256]{2,0,1:T(8,128)(2,1)}, u32[]{:S(2)}) copy-start(bf16[8,30,256]{2,0,1:T(8,128)(2,1)} %param.10) | copy-start | bytes 368644
  10.6 54.6 %all-to-all-start = ((bf16[8,30,3840]{2,1,0:T(8,128)(2,1)}), bf16[8,30,3840]{2,1,0:T(8,128)(2,1)S(1)}, u32[]{:S(2)}, u32[]{:S(2)}) async-start(bf16[8,30,3840]{2,1,0:T(8,128)(2,1)} %bitcast.1), calls=%async_computation | async-start | bytes 3932160 | tf_op jit(solution)/shard_map/all_to_all | solution.py:37
  66.7 78.2 %copy-start.4 = (bf16[40,8]{0,1:T(8,128)(2,1)S(1)}, bf16[40,8]{0,1:T(8,128)(2,1)}, u32[]{:S(2)}) copy-start(bf16[40,8]{0,1:T(8,128)(2,1)} %param.8) | copy-start | bytes 1924
  66.7 84.5 %copy-start.3 = (s32[40,8]{0,1:T(8,128)S(1)}, s32[40,8]{0,1:T(8,128)}, u32[]{:S(2)}) copy-start(s32[40,8]{0,1:T(8,128)} %param.7) | copy-start | bytes 3844
  137.6 13.4 %all-to-all-start.2 = ((f32[8,1,30]{2,1,0:T(1,128)}), f32[8,1,30]{2,1,0:T(1,128)S(1)}, u32[]{:S(2)}, u32[]{:S(2)}) async-start(f32[8,1,30]{2,1,0:T(1,128)} %all_to_all.18), calls=%async_computation.3 | async-start | bytes 8192 | tf_op jit(solution)/shard_map/all_to_all | solution.py:79
  144.9 226.7 %reduce-scatter.2.cloned.1.call-start = ((), (), s32[]{:S(2)}) async-start(), calls=%async_computation.4 | async-start | bytes 3973120 | tf_op jit(solution)/shard_map/reduce_scatter | solution.py:71
Sparse Core Ops, SparseCore 0:
  11.7 122.3 all-gather.1
  165.0 206.5 reduce-scatter.1
where the time goes:
time: 379 us; the launch traced here: 378 us
  waiting for transfers between devices  321 us (85%)
  starting transfers between devices  20.4 us (5%)
  between operations  14.1 us (4%)
  blocking collectives  10 us (3%)
  matrix products  5.98 us (2%)
  local copies, waits for them, and re-layouts  5.47 us (1%)
    reduce_scatter x1, waiting for transfers between devices, body(): lax.psum_scatter(lax.dot_general(columns, weighted, (((0,), (0,)), ((), (...  205 us
    all_gather x1, waiting for transfers between devices, body(): lax.all_gather(down_weight, 'dp', axis=0, tiled=True)  67.4 us
    all_to_all x1, waiting for transfers between devices, body(): lax.all_to_all(jnp.repeat(packed, sharing, axis=0), 'expert', split_axis=...  41.4 us
    all_to_all x1, starting transfers between devices, body(): lax.all_to_all(jnp.repeat(packed, sharing, axis=0), 'expert', split_axis=...  13.1 us
    all_to_all x1, blocking collectives, body(): lax.all_to_all(jnp.repeat(slot_prob, sharing, axis=0), 'expert', split_ax...  10 us
  transfers between devices with their start and end apart: 4, of which 4 were waited for; matrix products, arithmetic and copies ran while one was open for 2% of the time, Pallas kernels for 0%

commit v1 on v0

v1 whole, which is shorter than its diff:
```python
import functools

import jax
import jax.numpy as jnp
from jax import lax
from jax.experimental import pallas as pl
from jax.experimental.pallas import tpu as pltpu
from jax.sharding import PartitionSpec as P

FLIGHT = 2
NX = 4
H = 2
F32 = jnp.float32
BF16 = jnp.bfloat16


def kernel(
    cfg,
    tok_ref, route_ref, prob_ref, w_ref, gate_ref, up_ref,
    dg_ref, gg_ref, ug_ref, pg_ref,
    yb, meta, wt, gt, ut, pt, wo, wg, pb, cr, xs, xr, zs, zr, ac, vs, vr,
    y_send, y_recv, m_send, m_recv, wc_send, wc_recv, wz_send, wz_recv, wx_send, wx_recv,
    c_send, c_recv, x_send, x_recv, z_send, z_recv, v_send, v_recv,
):
    ny, nz = cfg
    toks, width = tok_ref.shape
    slots, hid = gate_ref.shape[1], gate_ref.shape[2]
    half = hid // 2
    nzh = nz // H
    chan = nzh * 2 * toks
    lanes = yb.shape[-1]
    n_chunks = NX * H

    d = lax.axis_index("dp")
    y = lax.axis_index("expert")
    x = lax.div(d, 2 * nz)
    z = lax.rem(lax.div(d, 2), nz)
    c = lax.rem(d, 2)
    expert0 = lax.div(y, ny // FLIGHT) == 0

    def at_x(i):
        return (lax.rem(x + i, NX) * nz + z) * 2 + c, y

    def at_z(zz):
        return (x * nz + zz) * 2 + c, y

    def at_y(i):
        return d, lax.rem(y + i, ny)

    other_core = ((x * nz + z) * 2 + (1 - c), y)

    def remote(src, dst, send, recv, to):
        return pltpu.make_async_remote_copy(
            src_ref=src, dst_ref=dst, send_sem=send, recv_sem=recv,
            device_id=to, device_id_type=pl.DeviceIdType.MESH,
        )

    barrier = pltpu.get_barrier_semaphore()
    partners = [other_core]
    partners += [at_x(i) for i in range(1, NX)]
    partners += [at_z(lax.rem(z + i, nz)) for i in range(1, nz)]
    partners += [at_y(i) for i in range(1, ny)]
    for to in partners:
        pl.semaphore_signal(barrier, inc=1, device_id=to, device_id_type=pl.DeviceIdType.MESH)

    sub = lax.broadcasted_iota(jnp.int32, (toks, 128), 0)
    lane = lax.broadcasted_iota(jnp.int32, (toks, 128), 1)
    eye = sub == lane

    def to_row(col):
        return jnp.sum(jnp.where(eye, col, 0.0), axis=0, keepdims=True)

    def to_col(row):
        return jnp.sum(jnp.where(eye, row, 0.0), axis=1, keepdims=True)

    route = route_ref[...]
    prob = prob_ref[...].astype(F32)
    rows = []
    for e in range(FLIGHT):
        hit = route == e
        on = jnp.sum(jnp.where(hit, 1.0, 0.0), axis=1, keepdims=True)
        weight = jnp.sum(jnp.where(hit, prob, 0.0), axis=1, keepdims=True)
        before = jnp.sum(jnp.where(lane < sub, to_row(on), 0.0), axis=1, keepdims=True)
        rows += [to_row(weight), to_row(jnp.where(on > 0.0, before, -1.0))]
    line = lax.broadcasted_iota(jnp.int32, (8, 128), 0)
    tile = jnp.zeros((8, 128), F32)
    for i, row in enumerate(rows):
        tile = jnp.where(line == i, row, tile)
    meta[y] = tile

    for k in range(NX):
        for h in range(H):
            pieces = []
            for i in range(nzh):
                start = ((k * nz) + i * H + h) * 2 * toks
                pieces.append(tok_ref[:, start:start + 2 * toks].astype(F32))
            if lanes > chan:
                pieces.append(jnp.zeros((toks, lanes - chan), F32))
            yb[k, h, y] = jnp.concatenate(pieces, axis=1).astype(BF16)

    pl.semaphore_wait(barrier, len(partners))

    def target_x(q):
        return lax.rem(x + 1 + q % NX, NX)

    def hops(q, way):
        return ny // 2 if (q + way) % 2 == 0 else ny // 2 - 1

    def ring(q, way, s):
        block = lax.rem(y + ny - s, ny) if way == 0 else lax.rem(y + s, ny)
        ref = yb.at[target_x(q), q // NX, block]
        return remote(
            ref, ref, y_send.at[q, way, s], y_recv.at[q, way, s], at_y(1 if way == 0 else ny - 1)
        )

    meta_copies = [
        remote(meta.at[y], meta.at[y], m_send.at[i - 1], m_recv.at[i - 1], at_y(i))
        for i in range(1, ny)
    ]
    w_pair = remote(w_ref, wo, wc_send.at[0], wc_recv.at[0], other_core)
    zh, zi = lax.rem(z, H), lax.div(z, H)
    w_own = wg.at[c, x, zh, zi]
    w_z = [
        remote(w_own, w_own, wz_send.at[i - 1], wz_recv.at[i - 1], at_z(lax.rem(z + i, nz)))
        for i in range(1, nz)
    ]
    w_x = [
        remote(wg.at[c, x], wg.at[c, x], wx_send.at[i], wx_recv.at[i], at_x(1 if i == 0 else NX - 1))
        for i in range(2)
    ]
    w_relay = []
    for i in range(2):
        ref = wg.at[c, lax.rem(x + (NX - 1 if i == 0 else 1), NX), i]
        w_relay.append(
            remote(ref, ref, wx_send.at[2 + i], wx_recv.at[2 + i], at_x(1 if i == 0 else NX - 1))
        )
    w_core = remote(wg.at[c], wg.at[c], wc_send.at[1], wc_recv.at[1], other_core)
    core_copies = [
        remote(pb.at[q, 1 - c], cr.at[q], c_send.at[q], c_recv.at[q], other_core)
        for q in range(n_chunks)
    ]
    x_copies = {
        q: remote(
            xs.at[q // NX, q % NX], xr.at[q // NX, q % NX],
            x_send.at[q // NX, q % NX], x_recv.at[q // NX, q % NX], at_x(1 + q % NX),
        )
        for q in range(n_chunks) if q % NX < NX - 1
    }
    value_copies = [
        remote(
            vs.at[lax.rem(y + i, ny)], vr.at[y], v_send.at[i - 1], v_recv.at[i - 1], at_y(i)
        )
        for i in range(1, ny)
    ]

    def z_copy(h, i):
        return remote(
            zs.at[h, i], zr.at[z], z_send.at[h, i], z_recv.at[z], at_z(i * H + h)
        )

    def row_of(source, field):
        both = meta[source]
        return jnp.where(expert0, both[field:field + 1], both[2 + field:3 + field])

    def spread():
        for copy in meta_copies:
            copy.wait_recv()
        for s in range(ny):
            slot_col = to_col(row_of(s, 1))
            p_col = to_col(row_of(s, 0))
            slot_lane = lax.broadcasted_iota(jnp.int32, (toks, slots), 1).astype(F32)
            table = jnp.where(slot_col == slot_lane, 1.0, 0.0).astype(BF16)
            g = jnp.dot(table, gate_ref[s], preferred_element_type=F32)
            u = jnp.dot(table, up_ref[s], preferred_element_type=F32)
            gt[s] = g
            ut[s] = u
            pt[s] = jnp.broadcast_to(p_col, (toks, 128))
            hidden = g * jax.nn.sigmoid(g) * u
            wt[pl.ds(s * toks, toks), :] = p_col * hidden

    def tokens_of(k, h):
        return yb[k, h].astype(F32).reshape(ny * toks, lanes).astype(BF16)

    def multiply(q):
        for way in range(2):
            if hops(q, way):
                ring(q, way, hops(q, way) - 1).wait_recv()
        part = lax.dot_general(
            tokens_of(target_x(q), q // NX), wt[...].astype(BF16), (((0,), (0,)), ((), ())),
            preferred_element_type=F32,
        )
        for i in range(nzh):
            for j in range(2):
                lo = (i * 2 + j) * toks
                pb[q, j, i] = part[lo:lo + toks]
        core_copies[q].start()

    def pair(q):
        h, j = q // NX, q % NX
        core_copies[q].wait_recv()
        total = pb[q, c] + cr[q]
        if j < NX - 1:
            xs[h, j] = total.astype(BF16)
            x_copies[q].start()
            return
        for i in range(NX - 1):
            x_copies[h * NX + i].wait_recv()
            total = total + xr[h, i].astype(F32)
        ac[h] = total
        zs[h] = total.astype(BF16)
        for i in range(nzh):
            @pl.when(z != i * H + h)
            def _():
                z_copy(h, i).start()

    def w_first():
        w_pair.wait_recv()
        mine = w_ref[...].astype(F32)
        theirs = wo[...].astype(F32)
        first = jnp.where(c == 0, mine, theirs)
        second = jnp.where(c == 0, theirs, mine)
        both = jnp.concatenate([first, second], axis=0)
        wg[c, x, zh, zi] = jnp.where(c == 0, both[:, :half], both[:, half:]).astype(BF16)
        for copy in w_z:
            copy.start()

    def w_second():
        for copy in w_z:
            copy.wait_recv()
        for copy in w_x:
            copy.start()

    def w_third():
        for copy, relay in zip(w_x, w_relay):
            copy.wait_recv()
            relay.start()

    def w_fourth():
        for relay in w_relay:
            relay.wait_recv()
        w_core.start()

    def activations():
        w_core.wait_recv()
        dh = jnp.zeros((ny * toks, hid), F32)
        for k in range(NX):
            for h in range(H):
                weights = jnp.concatenate(
                    [wg[i, k, h].reshape(chan, half) for i in range(2)], axis=1
                )
                dh = dh + jnp.dot(
                    tokens_of(k, h)[:, :chan], weights, preferred_element_type=F32
                )
        for s in range(ny):
            dh_s = dh[s * toks:(s + 1) * toks]
            g, u, p = gt[s], ut[s], pt[s][:, :1]
            sig = jax.nn.sigmoid(g)
            act = g * sig
            hidden = act * u
            scaled = p * dh_s
            up_tok = (scaled * act).astype(BF16)
            gate_tok = (scaled * u * sig * (1.0 + g * (1.0 - sig))).astype(BF16)
            slot_line = lax.broadcasted_iota(jnp.int32, (slots, toks), 0).astype(F32)
            pack = jnp.where(row_of(s, 1)[:, :toks] == slot_line, 1.0, 0.0).astype(BF16)
            ug_ref[s] = jnp.dot(pack, up_tok, preferred_element_type=F32).astype(BF16)
            gg_ref[s] = jnp.dot(pack, gate_tok, preferred_element_type=F32).astype(BF16)
            value = to_row(jnp.sum(hidden * dh_s, axis=1, keepdims=True))
            vs[s] = jnp.broadcast_to(value, (8, 128))
        for copy in value_copies:
            copy.start()
        vr[y] = vs[y]

    w_pair.start()
    for copy in meta_copies:
        copy.start()
    depth = ny // 2
    for way in range(2):
        if hops(0, way):
            ring(0, way, 0).start()
    for t in range(n_chunks + depth + 1):
        if t + 1 < n_chunks:
            for way in range(2):
                if hops(t + 1, way):
                    ring(t + 1, way, 0).start()
        if t == 0:
            w_first()
        for s in range(depth - 1, 0, -1):
            q = t - s
            if 0 <= q < n_chunks:
                for way in range(2):
                    if s < hops(q, way):
                        ring(q, way, s - 1).wait_recv()
                        ring(q, way, s).start()
        if t == 0:
            spread()
        if t == 3:
            w_second()
        if t == 6:
            w_third()
        if t == 8:
            w_fourth()
        q = t - depth
        if 0 <= q < n_chunks:
            multiply(q)
        q = t - depth - 1
        if 0 <= q < n_chunks:
            pair(q)
    activations()

    for copy in value_copies:
        copy.wait_recv()
    held = jnp.zeros((toks, route.shape[1]), F32)
    share = ny // FLIGHT
    for e in range(FLIGHT):
        row = vr[e * share][0:1]
        for i in range(1, share):
            row = row + vr[e * share + i][0:1]
        held = held + jnp.where(route == e, to_col(row), 0.0)
    pg_ref[...] = held

    total = ac[zh, zi]
    for i in range(1, nz):
        source = lax.rem(z + i, nz)
        remote(zs.at[0, 0], zr.at[source], z_send.at[0, 0], z_recv.at[source], other_core).wait_recv()
        total = total + zr[source].astype(F32)
    dg_ref[...] = total

    for q in range(n_chunks):
        for way in range(2):
            for s in range(hops(q, way)):
                ring(q, way, s).wait_send()
    for copy in (
        meta_copies + [w_pair] + w_z + w_x + w_relay + [w_core] + core_copies
        + list(x_copies.values()) + value_copies
    ):
        copy.wait_send()
    for h in range(H):
        for i in range(nzh):
            @pl.when(z != i * H + h)
            def _():
                z_copy(h, i).wait_send()


def body(grad_out, routing, probs, down_weight, gate_saved, up_saved):
    ny, n_dp = lax.axis_size("expert"), lax.axis_size("dp")
    nz = n_dp // (2 * NX)
    toks, width = grad_out.shape
    slots, hid = gate_saved.shape[1:]
    half = hid // 2
    nzh = nz // H
    chan = nzh * 2 * toks
    lanes = -(-chan // 128) * 128
    n_chunks = NX * H
    depth = ny // 2
    dma = pltpu.SemaphoreType.DMA
    vmem = pl.BlockSpec(memory_space=pltpu.VMEM)
    scratch = [
        pltpu.VMEM((NX, H, ny, toks, lanes), BF16),
        pltpu.VMEM((ny, 8, 128), F32),
        pltpu.VMEM((ny * toks, hid), F32),
        pltpu.VMEM((ny, toks, hid), F32),
        pltpu.VMEM((ny, toks, hid), F32),
        pltpu.VMEM((ny, toks, 128), F32),
        pltpu.VMEM((toks, hid), BF16),
        pltpu.VMEM((2, NX, H, nzh, 2 * toks, half), BF16),
        pltpu.VMEM((n_chunks, 2, nzh, toks, hid), F32),
        pltpu.VMEM((n_chunks, nzh, toks, hid), F32),
        pltpu.VMEM((H, NX - 1, nzh, toks, hid), BF16),
        pltpu.VMEM((H, NX - 1, nzh, toks, hid), BF16),
        pltpu.VMEM((H, nzh, toks, hid), BF16),
        pltpu.VMEM((nz, toks, hid), BF16),
        pltpu.VMEM((H, nzh, toks, hid), F32),
        pltpu.VMEM((ny, 8, 128), F32),
        pltpu.VMEM((ny, 8, 128), F32),
        dma((n_chunks, 2, depth)), dma((n_chunks, 2, depth)),
        dma((ny - 1,)), dma((ny - 1,)),
        dma((2,)), dma((2,)),
        dma((nz - 1,)), dma((nz - 1,)),
        dma((4,)), dma((4,)),
        dma((n_chunks,)), dma((n_chunks,)),
        dma((H, NX - 1)), dma((H, NX - 1)),
        dma((H, nzh)), dma((nz,)),
        dma((ny - 1,)), dma((ny - 1,)),
    ]
    return pl.pallas_call(
        functools.partial(kernel, (ny, nz)),
        out_shape=(
            jax.ShapeDtypeStruct(down_weight.shape, F32),
            jax.ShapeDtypeStruct(gate_saved.shape, BF16),
            jax.ShapeDtypeStruct(gate_saved.shape, BF16),
            jax.ShapeDtypeStruct(routing.shape, F32),
        ),
        in_specs=[vmem] * 6,
        out_specs=(vmem,) * 4,
        scratch_shapes=scratch,
        compiler_params=pltpu.CompilerParams(
            collective_id=0, has_side_effects=True, vmem_limit_bytes=48 * 1024 * 1024
        ),
    )(grad_out, routing, probs, down_weight, gate_saved, up_saved)


def solution(mesh):
    in_specs = (
        P(("dp", "expert"), None),
        P(("dp", "expert"), None),
        P(("dp", "expert"), None),
        P("dp", "expert"),
        P("dp", None, "expert"),
        P("dp", None, "expert"),
    )
    out_specs = (
        P("dp", "expert"),
        P("dp", None, "expert"),
        P("dp", None, "expert"),
        P(("dp", "expert"), None),
    )
    return jax.shard_map(body, mesh=mesh, in_specs=in_specs, out_specs=out_specs, check_vma=False)
```

time: 379 us -> 81 us (0.21)
  the two profiles are of different devices: /device:TPU:8 before, /device:TPU:66 now
where the time goes in v1:
time: 81 us; the launch traced here: 80.8 us
  Pallas kernels  74.6 us (92%)
  local copies, waits for them, and re-layouts  5.48 us (7%)
    pallas_call x1, Pallas kernels, body(): pl.pallas_call(functools.partial(kernel, (ny, nz)), out_shape=(jax.ShapeD...  74.6 us
    unnamed x11, local copies, waits for them, and re-layouts  3.38 us
    pallas_call x3, local copies, waits for them, and re-layouts, body(): pl.pallas_call(functools.partial(kernel, (ny, nz)), out_shape=(jax.ShapeD...  2.1 us

profile of v1, /device:TPU:66, one launch (start us, length us, event | category | flops | bytes accessed | tf_op | source)
XLA Modules:
  0.0 80.8 jit_solution(16501047297569900736)
XLA Ops:
  0.6 0.0 copy-start.2
  0.6 0.0 copy-start
  0.7 0.8 %copy.11.prob_ref = bf16[40,8]{1,0:T(8,128)(2,1)S(1)} copy(bf16[40,8]{0,1:T(8,128)(2,1)} %param.8) | data formatting | bytes 1280 | tf_op args[2]
  1.5 0.0 copy-done.2
  1.5 0.1 copy.10.route_ref
  1.5 0.9 %copy.12.gate_ref = bf16[8,30,256]{2,1,0:T(8,128)(2,1)S(1)} copy(bf16[8,30,256]{2,0,1:T(8,128)(2,1)} %param.10) | data formatting | bytes 245760 | tf_op args[4]
  2.5 0.0 copy-start.1
  2.5 0.9 %copy.13.up_ref = bf16[8,30,256]{2,1,0:T(8,128)(2,1)S(1)} copy(bf16[8,30,256]{2,0,1:T(8,128)(2,1)} %param.11) | data formatting | bytes 245760 | tf_op args[5]
  3.4 0.0 copy-done
  3.4 0.0 copy-done.1
  3.4 74.6 %shard_map.93 = (f32[40,256]{1,0:T(8,128)S(1)}, bf16[8,30,256]{2,1,0:T(8,128)(2,1)S(1)}, bf16[8,30,256]{2,1,0:T(8,128)(2,1)S(1)}, f32[40,8]{1,0:T(8,128)S(1)}) custom-call(bf16[40,3840]{1,0:T(8,128)(2,1)S(1)} %copy-done, s32[40,8]{1,0:T(8,128)S(1)} %copy.10.route_ref, bf16[40,8]{1,0:T(8,128)(2,1)S(1)} %copy.11.prob_ref, bf16[40,256]{1,0:T(8,128)(2,1)S(1)} %copy-done.1, ...), custom_call_target="tpu_custom_call" | custom-call | tf_op jit(solution)/shard_map/pallas_call | solution.py:385
  78.0 0.7 copy.16
  78.7 0.7 copy.14
  79.4 0.7 copy.15
  80.1 0.6 copy.18
Async XLA Ops:
  0.6 0.8 %copy-start.2 = (s32[40,8]{0,1:T(8,128)S(1)}, s32[40,8]{0,1:T(8,128)}, u32[]{:S(2)}) copy-start(s32[40,8]{0,1:T(8,128)} %param.7) | copy-start | bytes 3844
  0.6 2.8 %copy-start = (bf16[40,3840]{1,0:T(8,128)(2,1)S(1)}, bf16[40,3840]{1,0:T(8,128)(2,1)}, u32[]{:S(2)}) copy-start(bf16[40,3840]{1,0:T(8,128)(2,1)} %tok_ref.1) | copy-start | bytes 921604
  2.5 1.0 %copy-start.1 = (bf16[40,256]{1,0:T(8,128)(2,1)S(1)}, bf16[40,256]{1,0:T(8,128)(2,1)}, u32[]{:S(2)}) copy-start(bf16[40,256]{1,0:T(8,128)(2,1)} %w_ref.1) | copy-start | bytes 61444

commit v2 on v1

--- a/solution.py
+++ b/solution.py
@@ -10,21 +10,23 @@
 FLIGHT = 2
 NX = 4
 H = 2
+G = 3
 F32 = jnp.float32
 BF16 = jnp.bfloat16
 
 
 def kernel(
     cfg,
-    tok_ref, route_ref, prob_ref, w_ref, gate_ref, up_ref,
+    tok_in, route_in, prob_in, w_in, gate_in, up_in,
     dg_ref, gg_ref, ug_ref, pg_ref,
+    tok_ref, route_ref, prob_ref, w_ref, gate_ref, up_ref, fetch,
     yb, meta, wt, gt, ut, pt, wo, wg, pb, cr, xs, xr, zs, zr, ac, vs, vr,
-    y_send, y_recv, m_send, m_recv, wc_send, wc_recv, wz_send, wz_recv, wx_send, wx_recv,
+    y_send, y_recv, m_send, m_recv, wc_send, wc_recv, wf_send, wf_recv, wz_send, wz_recv, wx_send, wx_recv,
     c_send, c_recv, x_send, x_recv, z_send, z_recv, v_send, v_recv,
 ):
     ny, nz = cfg
-    toks, width = tok_ref.shape
-    slots, hid = gate_ref.shape[1], gate_ref.shape[2]
+    toks, width = tok_in.shape
+    slots, hid = gate_in.shape[0], gate_in.shape[2]
     half = hid // 2
     nzh = nz // H
     chan = nzh * 2 * toks
@@ -54,6 +56,15 @@
             src_ref=src, dst_ref=dst, send_sem=send, recv_sem=recv,
             device_id=to, device_id_type=pl.DeviceIdType.MESH,
         )
+
+    fetched = {}
+    pairs = (
+        (tok_in, tok_ref), (route_in, route_ref), (prob_in, prob_ref), (w_in, w_ref),
+        (gate_in, gate_ref), (up_in, up_ref),
+    )
+    for i, (src, dst) in enumerate(pairs):
+        fetched[i] = pltpu.make_async_copy(src, dst, fetch.at[i])
+        fetched[i].start()
 
     barrier = pltpu.get_barrier_semaphore()
     partners = [other_core]
@@ -63,8 +74,8 @@
     for to in partners:
         pl.semaphore_signal(barrier, inc=1, device_id=to, device_id_type=pl.DeviceIdType.MESH)
 
-    sub = lax.broadcasted_iota(jnp.int32, (toks, 128), 0)
-    lane = lax.broadcasted_iota(jnp.int32, (toks, 128), 1)
+    sub = lax.broadcasted_iota(jnp.int32, (toks, toks), 0)
+    lane = lax.broadcasted_iota(jnp.int32, (toks, toks), 1)
     eye = sub == lane
 
     def to_row(col):
@@ -73,23 +84,26 @@
     def to_col(row):
         return jnp.sum(jnp.where(eye, row, 0.0), axis=1, keepdims=True)
 
+    fetched[1].wait()
+    fetched[2].wait()
     route = route_ref[...]
     prob = prob_ref[...].astype(F32)
     rows = []
     for e in range(FLIGHT):
         hit = route == e
-        on = jnp.sum(jnp.where(hit, 1.0, 0.0), axis=1, keepdims=True)
-        weight = jnp.sum(jnp.where(hit, prob, 0.0), axis=1, keepdims=True)
-        before = jnp.sum(jnp.where(lane < sub, to_row(on), 0.0), axis=1, keepdims=True)
-        rows += [to_row(weight), to_row(jnp.where(on > 0.0, before, -1.0))]
-    line = lax.broadcasted_iota(jnp.int32, (8, 128), 0)
-    tile = jnp.zeros((8, 128), F32)
+        on = jnp.sum(jnp.where(hit, 1.0, 0.0), axis=0, keepdims=True)
+        weight = jnp.sum(jnp.where(hit, prob, 0.0), axis=0, keepdims=True)
+        before = jnp.sum(jnp.where(sub < lane, to_col(on), 0.0), axis=0, keepdims=True)
+        rows += [weight, jnp.where(on > 0.0, before, -1.0)]
+    line = lax.broadcasted_iota(jnp.int32, (8, toks), 0)
+    tile = jnp.zeros((8, toks), F32)
     for i, row in enumerate(rows):
         tile = jnp.where(line == i, row, tile)
-    meta[y] = tile
-
-    for k in range(NX):
-        for h in range(H):
+    meta[y] = jnp.zeros((8, 128), F32)
+    meta[y, :, :toks] = tile
+
+    def arrange(h):
+        for k in range(NX):
             pieces = []
             for i in range(nzh):
                 start = ((k * nz) + i * H + h) * 2 * toks
@@ -98,6 +112,8 @@
                 pieces.append(jnp.zeros((toks, lanes - chan), F32))
             yb[k, h, y] = jnp.concatenate(pieces, axis=1).astype(BF16)
 
+    fetched[0].wait()
+    arrange(0)
     pl.semaphore_wait(barrier, len(partners))
 
     def target_x(q):
@@ -119,10 +135,15 @@
     ]
     w_pair = remote(w_ref, wo, wc_send.at[0], wc_recv.at[0], other_core)
     zh, zi = lax.rem(z, H), lax.div(z, H)
-    w_own = wg.at[c, x, zh, zi]
-    w_z = [
-        remote(w_own, w_own, wz_send.at[i - 1], wz_recv.at[i - 1], at_z(lax.rem(z + i, nz)))
-        for i in range(1, nz)
+    w_own = wg.at[c, x, lax.rem(z, G), lax.div(z, G)]
+    w_far = [
+        remote(w_own, w_own, wf_send.at[i - 1], wf_recv.at[i - 1], at_z(lax.rem(z + i * G, nz)))
+        for i in range(1, nz // G)
+    ]
+    w_class = wg.at[c, x, lax.rem(z, G)]
+    w_near = [
+        remote(w_class, w_class, wz_send.at[i], wz_recv.at[i], at_z(lax.rem(z + (1 if i == 0 else nz - 1), nz)))
+        for i in range(2)
     ]
     w_x = [
         remote(wg.at[c, x], wg.at[c, x], wx_send.at[i], wx_recv.at[i], at_x(1 if i == 0 else NX - 1))
@@ -130,7 +151,7 @@
     ]
     w_relay = []
     for i in range(2):
-        ref = wg.at[c, lax.rem(x + (NX - 1 if i == 0 else 1), NX), i]
+        ref = wg.at[c, lax.rem(x + (NX - 1 if i == 0 else 1), NX), :, pl.ds(i * (nz // G // 2), nz // G // 2)]
         w_relay.append(
             remote(ref, ref, wx_send.at[2 + i], wx_recv.at[2 + i], at_x(1 if i == 0 else NX - 1))
         )
@@ -159,24 +180,32 @@
         )
 
     def row_of(source, field):
-        both = meta[source]
+        both = meta[source][:, :toks]
         return jnp.where(expert0, both[field:field + 1], both[2 + field:3 + field])
 
     def spread():
+        fetched[4].wait()
+        fetched[5].wait()
         for copy in meta_copies:
             copy.wait_recv()
+        tables = []
         for s in range(ny):
             slot_col = to_col(row_of(s, 1))
             p_col = to_col(row_of(s, 0))
-            slot_lane = lax.broadcasted_iota(jnp.int32, (toks, slots), 1).astype(F32)
-            table = jnp.where(slot_col == slot_lane, 1.0, 0.0).astype(BF16)
-            g = jnp.dot(table, gate_ref[s], preferred_element_type=F32)
-            u = jnp.dot(table, up_ref[s], preferred_element_type=F32)
-            gt[s] = g
-            ut[s] = u
-            pt[s] = jnp.broadcast_to(p_col, (toks, 128))
-            hidden = g * jax.nn.sigmoid(g) * u
-            wt[pl.ds(s * toks, toks), :] = p_col * hidden
+            place = lax.broadcasted_iota(jnp.int32, (toks, slots * ny), 1)
+            mine = (lax.rem(place, ny) == s) & (lax.div(place, ny).astype(F32) == slot_col)
+            tables.append(jnp.where(mine, 1.0, 0.0))
+            pt[pl.ds(s * toks, toks), :] = jnp.broadcast_to(p_col, (toks, 128))
+        table = jnp.concatenate(tables, axis=0).astype(BF16)
+        g = jnp.dot(table, saved(gate_ref), preferred_element_type=F32)
+        u = jnp.dot(table, saved(up_ref), preferred_element_type=F32)
+        gt[...] = g
+        ut[...] = u
+        hidden = g * jax.nn.sigmoid(g) * u
+        wt[...] = (pt[:, :1] * hidden).astype(BF16)
+
+    def saved(ref):
+        return ref[...].astype(F32).reshape(slots * ny, hid).astype(BF16)
 
     def tokens_of(k, h):
         return yb[k, h].astype(F32).reshape(ny * toks, lanes).astype(BF16)
@@ -186,7 +215,7 @@
             if hops(q, way):
                 ring(q, way, hops(q, way) - 1).wait_recv()
         part = lax.dot_general(
-            tokens_of(target_x(q), q // NX), wt[...].astype(BF16), (((0,), (0,)), ((), ())),
+            tokens_of(target_x(q), q // NX), wt[...], (((0,), (0,)), ((), ())),
             preferred_element_type=F32,
         )
         for i in range(nzh):
@@ -220,12 +249,18 @@
         first = jnp.where(c == 0, mine, theirs)
         second = jnp.where(c == 0, theirs, mine)
         both = jnp.concatenate([first, second], axis=0)
-        wg[c, x, zh, zi] = jnp.where(c == 0, both[:, :half], both[:, half:]).astype(BF16)
-        for copy in w_z:
+        wg[c, x, lax.rem(z, G), lax.div(z, G)] = jnp.where(c == 0, both[:, :half], both[:, half:]).astype(BF16)
+        for copy in w_far:
             copy.start()
 
+    def w_near_step():
+        for copy in w_far:
+            copy.wait_recv()
+        for copy in w_near:
+            copy.start()
+
     def w_second():
-        for copy in w_z:
+        for copy in w_near:
             copy.wait_recv()
         for copy in w_x:
             copy.start()
@@ -246,30 +281,42 @@
         for k in range(NX):
             for h in range(H):
                 weights = jnp.concatenate(
-                    [wg[i, k, h].reshape(chan, half) for i in range(2)], axis=1
+                    [
+                        jnp.concatenate(
+                            [wg[i, k, zz % G, zz // G] for zz in range(h, nz, H)], axis=0
+                        )
+                        for i in range(2)
+                    ],
+                    axis=1,
                 )
                 dh = dh + jnp.dot(
                     tokens_of(k, h)[:, :chan], weights, preferred_element_type=F32
                 )
+        g, u, p = gt[...], ut[...], pt[:, :1]
+        sig = jax.nn.sigmoid(g)
+        act = g * sig
+        hidden = act * u
+        scaled = p * dh
+        up_tok = (scaled * act).astype(BF16)
+        gate_tok = (scaled * u * sig * (1.0 + g * (1.0 - sig))).astype(BF16)
+        value = jnp.sum(hidden * dh, axis=1, keepdims=True)
         for s in range(ny):
-            dh_s = dh[s * toks:(s + 1) * toks]
-            g, u, p = gt[s], ut[s], pt[s][:, :1]
-            sig = jax.nn.sigmoid(g)
-            act = g * sig
-            hidden = act * u
-            scaled = p * dh_s
-            up_tok = (scaled * act).astype(BF16)
-            gate_tok = (scaled * u * sig * (1.0 + g * (1.0 - sig))).astype(BF16)
-            slot_line = lax.broadcasted_iota(jnp.int32, (slots, toks), 0).astype(F32)
-            pack = jnp.where(row_of(s, 1)[:, :toks] == slot_line, 1.0, 0.0).astype(BF16)
-            ug_ref[s] = jnp.dot(pack, up_tok, preferred_element_type=F32).astype(BF16)
-            gg_ref[s] = jnp.dot(pack, gate_tok, preferred_element_type=F32).astype(BF16)
-            value = to_row(jnp.sum(hidden * dh_s, axis=1, keepdims=True))
-            vs[s] = jnp.broadcast_to(value, (8, 128))
+            row = to_row(value[s * toks:(s + 1) * toks])
+            vs[s, :, :toks] = jnp.broadcast_to(row, (8, toks))
         for copy in value_copies:
             copy.start()
         vr[y] = vs[y]
-
+        packs = []
+        for s in range(ny):
+            place = lax.broadcasted_iota(jnp.int32, (slots * ny, toks), 0)
+            mine = (lax.rem(place, ny) == s) & (lax.div(place, ny).astype(F32) == row_of(s, 1))
+            packs.append(jnp.where(mine, 1.0, 0.0))
+        pack = jnp.concatenate(packs, axis=1).astype(BF16)
+        for ref, values in ((ug_ref, up_tok), (gg_ref, gate_tok)):
+            packed = jnp.dot(pack, values, preferred_element_type=F32)
+            ref[...] = packed.reshape(slots, ny, hid).astype(BF16)
+
+    fetched[3].wait()
     w_pair.start()
     for copy in meta_copies:
         copy.start()
@@ -277,14 +324,13 @@
     for way in range(2):
         if hops(0, way):
             ring(0, way, 0).start()
+    arrange(1)
     for t in range(n_chunks + depth + 1):
         if t + 1 < n_chunks:
             for way in range(2):
                 if hops(t + 1, way):
                     ring(t + 1, way, 0).start()
-        if t == 0:
-            w_first()
-        for s in range(depth - 1, 0, -1):
+        for s in range(1, depth):
             q = t - s
             if 0 <= q < n_chunks:
                 for way in range(2):
@@ -292,12 +338,15 @@
                         ring(q, way, s - 1).wait_recv()
                         ring(q, way, s).start()
         if t == 0:
+            w_first()
             spread()
-        if t == 3:
+        if t == 2:
+            w_near_step()
+        if t == 4:
             w_second()
         if t == 6:
             w_third()
-        if t == 8:
+        if t == 7:
             w_fourth()
         q = t - depth
         if 0 <= q < n_chunks:
@@ -309,13 +358,13 @@
 
     for copy in value_copies:
         copy.wait_recv()
-    held = jnp.zeros((toks, route.shape[1]), F32)
+    held = jnp.zeros(route.shape, F32)
     share = ny // FLIGHT
     for e in range(FLIGHT):
-        row = vr[e * share][0:1]
+        row = vr[e * share][0:1, :toks]
         for i in range(1, share):
-            row = row + vr[e * share + i][0:1]
-        held = held + jnp.where(route == e, to_col(row), 0.0)
+            row = row + vr[e * share + i][0:1, :toks]
+        held = held + jnp.where(route == e, row, 0.0)
     pg_ref[...] = held
 
     total = ac[zh, zi]
@@ -330,7 +379,7 @@
             for s in range(hops(q, way)):
                 ring(q, way, s).wait_send()
     for copy in (
-        meta_copies + [w_pair] + w_z + w_x + w_relay + [w_core] + core_copies
+        meta_copies + [w_pair] + w_far + w_near + w_x + w_relay + [w_core] + core_copies
         + list(x_copies.values()) + value_copies
     ):
         copy.wait_send()
@@ -341,11 +390,24 @@
                 z_copy(h, i).wait_send()
 
 
+def hand_over(a, b, c, d, a_out, b_out, c_out, d_out, sem):
+    copies = [
+        pltpu.make_async_copy(src, dst, sem.at[i])
+        for i, (src, dst) in enumerate(((a, a_out), (b, b_out), (c, c_out), (d, d_out)))
+    ]
+    for copy in copies:
+        copy.start()
+    for copy in copies:
+        copy.wait()
+
+
 def body(grad_out, routing, probs, down_weight, gate_saved, up_saved):
     ny, n_dp = lax.axis_size("expert"), lax.axis_size("dp")
     nz = n_dp // (2 * NX)
     toks, width = grad_out.shape
     slots, hid = gate_saved.shape[1:]
+    saved = (slots, ny, hid)
+    top = routing.shape[1]
     half = hid // 2
     nzh = nz // H
     chan = nzh * 2 * toks
@@ -355,14 +417,21 @@
     dma = pltpu.SemaphoreType.DMA
     vmem = pl.BlockSpec(memory_space=pltpu.VMEM)
     scratch = [
+        pltpu.VMEM(grad_out.shape, BF16),
+        pltpu.VMEM((top, toks), jnp.int32),
+        pltpu.VMEM((top, toks), BF16),
+        pltpu.VMEM(down_weight.shape, BF16),
+        pltpu.VMEM(saved, BF16),
+        pltpu.VMEM(saved, BF16),
+        dma((6,)),
         pltpu.VMEM((NX, H, ny, toks, lanes), BF16),
         pltpu.VMEM((ny, 8, 128), F32),
+        pltpu.VMEM((ny * toks, hid), BF16),
         pltpu.VMEM((ny * toks, hid), F32),
-        pltpu.VMEM((ny, toks, hid), F32),
-        pltpu.VMEM((ny, toks, hid), F32),
-        pltpu.VMEM((ny, toks, 128), F32),
+        pltpu.VMEM((ny * toks, hid), F32),
+        pltpu.VMEM((ny * toks, 128), F32),
         pltpu.VMEM((toks, hid), BF16),
-        pltpu.VMEM((2, NX, H, nzh, 2 * toks, half), BF16),
+        pltpu.VMEM((2, NX, G, nz // G, 2 * toks, half), BF16),
         pltpu.VMEM((n_chunks, 2, nzh, toks, hid), F32),
         pltpu.VMEM((n_chunks, nzh, toks, hid), F32),
         pltpu.VMEM((H, NX - 1, nzh, toks, hid), BF16),
@@ -375,28 +444,45 @@
         dma((n_chunks, 2, depth)), dma((n_chunks, 2, depth)),
         dma((ny - 1,)), dma((ny - 1,)),
         dma((2,)), dma((2,)),
-        dma((nz - 1,)), dma((nz - 1,)),
+        dma((nz // G - 1,)), dma((nz // G - 1,)),
+        dma((2,)), dma((2,)),
         dma((4,)), dma((4,)),
         dma((n_chunks,)), dma((n_chunks,)),
         dma((H, NX - 1)), dma((H, NX - 1)),
         dma((H, nzh)), dma((nz,)),
         dma((ny - 1,)), dma((ny - 1,)),
     ]
-    return pl.pallas_call(
+    shapes = (
+        jax.ShapeDtypeStruct(down_weight.shape, F32),
+        jax.ShapeDtypeStruct(saved, BF16),
+        jax.ShapeDtypeStruct(saved, BF16),
+        jax.ShapeDtypeStruct((top, toks), F32),
+    )
+    parts = pl.pallas_call(
         functools.partial(kernel, (ny, nz)),
-        out_shape=(
-            jax.ShapeDtypeStruct(down_weight.shape, F32),
-            jax.ShapeDtypeStruct(gate_saved.shape, BF16),
-            jax.ShapeDtypeStruct(gate_saved.shape, BF16),
-            jax.ShapeDtypeStruct(routing.shape, F32),
-        ),
-        in_specs=[vmem] * 6,
+        out_shape=shapes,
+        in_specs=[pl.BlockSpec(memory_space=pl.ANY)] * 6,
         out_specs=(vmem,) * 4,
         scratch_shapes=scratch,
         compiler_params=pltpu.CompilerParams(
-            collective_id=0, has_side_effects=True, vmem_limit_bytes=48 * 1024 * 1024
+            collective_id=0, has_side_effects=True, vmem_limit_bytes=63 * 1024 * 1024
         ),
-    )(grad_out, routing, probs, down_weight, gate_saved, up_saved)
+    )(
+        grad_out, routing.T, probs.T, down_weight,
+        jnp.transpose(gate_saved, (1, 0, 2)), jnp.transpose(up_saved, (1, 0, 2)),
+    )
+    down_grad, gate_grad, up_grad, prob_grad = pl.pallas_call(
+        hand_over,
+        out_shape=shapes,
+        in_specs=[pl.BlockSpec(memory_space=pl.ANY)] * 4,
+        out_specs=(pl.BlockSpec(memory_space=pl.ANY),) * 4,
+        scratch_shapes=[dma((4,))],
+        compiler_params=pltpu.CompilerParams(vmem_limit_bytes=63 * 1024 * 1024),
+    )(*parts)
+    return (
+        down_grad, jnp.transpose(gate_grad, (1, 0, 2)), jnp.transpose(up_grad, (1, 0, 2)),
+        prob_grad.T,
+    )
 
 
 def solution(mesh):

time: 81 us -> 83.3 us (1.028)
  Pallas kernels: 74.6 us -> 82.5 us
  local copies, waits for them, and re-layouts: 5.48 us -> 0 us
    pallas_call x1 -> x2, Pallas kernels: 74.6 us -> 82.5 us  [the longest x1 72.5 us: body(): pl.pallas_call(functools.partial(kernel, (ny, nz)), out_shape=shapes, in_...]
    unnamed x11 -> x0, local copies, waits for them, and re-layouts: 3.38 us -> none
    pallas_call x3 -> x0, local copies, waits for them, and re-layouts: 2.1 us -> none  [body(): pl.pallas_call(functools.partial(kernel, (ny, nz)), out_shape=(jax.ShapeD...]
where the time goes in v2:
time: 83.3 us; the launch traced here: 83.1 us
  Pallas kernels  82.5 us (99%)
    pallas_call x1, Pallas kernels, body(): pl.pallas_call(functools.partial(kernel, (ny, nz)), out_shape=shapes, in_...  72.5 us
    pallas_call x1, Pallas kernels, body(): pl.pallas_call(hand_over, out_shape=shapes, in_specs=[pl.BlockSpec(memory...  9.95 us

profile of v2, /device:TPU:66, one launch (start us, length us, event | category | flops | bytes accessed | tf_op | source)
XLA Modules:
  0.0 83.1 jit_solution(4729075257577193719)
XLA Ops:
  0.6 72.5 %shard_map.93 = (f32[40,256]{1,0:T(8,128)}, bf16[30,8,256]{2,1,0:T(8,128)(2,1)}, bf16[30,8,256]{2,1,0:T(8,128)(2,1)}, f32[8,40]{1,0:T(8,128)}) custom-call(bf16[40,3840]{1,0:T(8,128)(2,1)} %tok_in.1, s32[8,40]{1,0:T(8,128)} %bitcast.9, bf16[8,40]{1,0:T(8,128)(2,1)} %bitcast.10, bf16[40,256]{1,0:T(8,128)(2,1)} %w_in.1, bf16[30,8,256]{2,1,0:T(8,128)(2,1)} %bitcast.7, ...), custom_call_target="tpu_custom_call" | custom-call | tf_op jit(solution)/shard_map/pallas_call | solution.py:461
  73.2 9.9 %shard_map.94 = (f32[40,256]{1,0:T(8,128)}, bf16[30,8,256]{2,1,0:T(8,128)(2,1)}, bf16[30,8,256]{2,1,0:T(8,128)(2,1)}, f32[8,40]{1,0:T(8,128)}) custom-call(f32[40,256]{1,0:T(8,128)} %get-tuple-element.12.a, bf16[30,8,256]{2,1,0:T(8,128)(2,1)} %get-tuple-element.13.b, bf16[30,8,256]{2,1,0:T(8,128)(2,1)} %get-tuple-element.14.c, f32[8,40]{1,0:T(8,128)} %get-tuple-element.15.d), custom_call_target="tpu_custom_call" | custom-call | tf_op jit(solution)/shard_map/pallas_call | solution.py:474

commit v3 on v2

--- a/solution.py
+++ b/solution.py
@@ -11,6 +11,12 @@
 NX = 4
 H = 2
 G = 3
+SKEW = 2
+AHEAD = 3
+LAG = 2
+WAIT_X = 2
+SPREAD = 2
+W_SLOTS = (1, 4, 6, 9, 11)
 F32 = jnp.float32
 BF16 = jnp.bfloat16
 
@@ -231,7 +237,11 @@
         if j < NX - 1:
             xs[h, j] = total.astype(BF16)
             x_copies[q].start()
-            return
+        else:
+            ac[h] = total
+
+    def finish(h):
+        total = ac[h]
         for i in range(NX - 1):
             x_copies[h * NX + i].wait_recv()
             total = total + xr[h, i].astype(F32)
@@ -318,43 +328,40 @@
 
     fetched[3].wait()
     w_pair.start()
-    for copy in meta_copies:
-        copy.start()
     depth = ny // 2
-    for way in range(2):
-        if hops(0, way):
-            ring(0, way, 0).start()
-    arrange(1)
-    for t in range(n_chunks + depth + 1):
-        if t + 1 < n_chunks:
-            for way in range(2):
-                if hops(t + 1, way):
-                    ring(t + 1, way, 0).start()
+    work = {0: [lambda: arrange(1)], SPREAD: [spread]}
+    for slot, step in zip(W_SLOTS, (w_first, w_near_step, w_second, w_third, w_fourth)):
+        work.setdefault(slot, []).append(step)
+    last = n_chunks - 1 + SKEW * (depth - 1) + LAG
+    for t in range(last + 1):
+        for q in range(n_chunks):
+            if max(0, q - AHEAD) == t:
+                for way in range(2):
+                    if hops(q, way):
+                        ring(q, way, 0).start()
+        if t == 0:
+            for copy in meta_copies:
+                copy.start()
         for s in range(1, depth):
-            q = t - s
+            q = t - SKEW * (s - 1)
             if 0 <= q < n_chunks:
                 for way in range(2):
                     if s < hops(q, way):
                         ring(q, way, s - 1).wait_recv()
                         ring(q, way, s).start()
-        if t == 0:
-            w_first()
-            spread()
-        if t == 2:
-            w_near_step()
-        if t == 4:
-            w_second()
-        if t == 6:
-            w_third()
-        if t == 7:
-            w_fourth()
-        q = t - depth
+        for step in work.get(t, []):
+            step()
+        q = t - SKEW * (depth - 1)
         if 0 <= q < n_chunks:
             multiply(q)
-        q = t - depth - 1
+        q = t - SKEW * (depth - 1) - LAG
         if 0 <= q < n_chunks:
+            if q == n_chunks - 1:
+                activations()
             pair(q)
-    activations()
+        if t == NX - 1 + SKEW * (depth - 1) + LAG + WAIT_X:
+            finish(0)
+    finish(1)
 
     for copy in value_copies:
         copy.wait_recv()
@@ -390,15 +397,9 @@
                 z_copy(h, i).wait_send()
 
 
-def hand_over(a, b, c, d, a_out, b_out, c_out, d_out, sem):
-    copies = [
-        pltpu.make_async_copy(src, dst, sem.at[i])
-        for i, (src, dst) in enumerate(((a, a_out), (b, b_out), (c, c_out), (d, d_out)))
-    ]
-    for copy in copies:
-        copy.start()
-    for copy in copies:
-        copy.wait()
+def hand_over(a, b, c, d, a_out, b_out, c_out, d_out):
+    for src, dst in ((a, a_out), (b, b_out), (c, c_out), (d, d_out)):
+        dst[...] = src[...]
 
 
 def body(grad_out, routing, probs, down_weight, gate_saved, up_saved):
@@ -474,9 +475,8 @@
     down_grad, gate_grad, up_grad, prob_grad = pl.pallas_call(
         hand_over,
         out_shape=shapes,
-        in_specs=[pl.BlockSpec(memory_space=pl.ANY)] * 4,
-        out_specs=(pl.BlockSpec(memory_space=pl.ANY),) * 4,
-        scratch_shapes=[dma((4,))],
+        in_specs=[vmem] * 4,
+        out_specs=(vmem,) * 4,
         compiler_params=pltpu.CompilerParams(vmem_limit_bytes=63 * 1024 * 1024),
     )(*parts)
     return (

time: 83.3 us -> 70.2 us (0.84)
  Pallas kernels: 82.5 us -> 69.2 us
    pallas_call x1, Pallas kernels: 9.95 us -> 1.7 us  [body(): pl.pallas_call(hand_over, out_shape=shapes, in_specs=[vmem] * 4, out_spec...]
    pallas_call x1, Pallas kernels: 72.5 us -> 67.5 us  [body(): pl.pallas_call(functools.partial(kernel, (ny, nz)), out_shape=shapes, in_...]
where the time goes in v3:
time: 70.2 us; the launch traced here: 69.8 us
  Pallas kernels  69.2 us (99%)
    pallas_call x1, Pallas kernels, body(): pl.pallas_call(functools.partial(kernel, (ny, nz)), out_shape=shapes, in_...  67.5 us
    pallas_call x1, Pallas kernels, body(): pl.pallas_call(hand_over, out_shape=shapes, in_specs=[vmem] * 4, out_spec...  1.7 us

profile of v3, /device:TPU:66, one launch (start us, length us, event | category | flops | bytes accessed | tf_op | source)
XLA Modules:
  0.0 69.8 jit_solution(1528037659180081213)
XLA Ops:
  0.6 67.5 %shard_map.93 = (f32[40,256]{1,0:T(8,128)}, bf16[30,8,256]{2,1,0:T(8,128)(2,1)}, bf16[30,8,256]{2,1,0:T(8,128)(2,1)}, f32[8,40]{1,0:T(8,128)}) custom-call(bf16[40,3840]{1,0:T(8,128)(2,1)} %tok_in.1, s32[8,40]{1,0:T(8,128)} %bitcast.9, bf16[8,40]{1,0:T(8,128)(2,1)} %bitcast.10, bf16[40,256]{1,0:T(8,128)(2,1)} %w_in.1, bf16[30,8,256]{2,1,0:T(8,128)(2,1)} %bitcast.7, ...), custom_call_target="tpu_custom_call" | custom-call | tf_op jit(solution)/shard_map/pallas_call | solution.py:462
  68.1 1.7 %shard_map.94 = (f32[40,256]{1,0:T(8,128)}, bf16[30,8,256]{2,1,0:T(8,128)(2,1)}, bf16[30,8,256]{2,1,0:T(8,128)(2,1)}, f32[8,40]{1,0:T(8,128)}) custom-call(f32[40,256]{1,0:T(8,128)} %get-tuple-element.12.a, bf16[30,8,256]{2,1,0:T(8,128)(2,1)} %get-tuple-element.13.b, bf16[30,8,256]{2,1,0:T(8,128)(2,1)} %get-tuple-element.14.c, f32[8,40]{1,0:T(8,128)} %get-tuple-element.15.d), custom_call_target="tpu_custom_call" | custom-call | tf_op jit(solution)/shard_map/pallas_call | solution.py:475

commit v4 on v3

--- a/solution.py
+++ b/solution.py
@@ -9,14 +9,14 @@
 
 FLIGHT = 2
 NX = 4
-H = 2
+H = 4
 G = 3
-SKEW = 2
-AHEAD = 3
-LAG = 2
-WAIT_X = 2
-SPREAD = 2
-W_SLOTS = (1, 4, 6, 9, 11)
+SKEW = 3
+AHEAD = 5
+LAG = 3
+WAIT_X = 4
+SPREAD = 4
+W_SLOTS = (2, 8, 12, 17, 21)
 F32 = jnp.float32
 BF16 = jnp.bfloat16
 
@@ -119,7 +119,8 @@
             yb[k, h, y] = jnp.concatenate(pieces, axis=1).astype(BF16)
 
     fetched[0].wait()
-    arrange(0)
+    for h in range(H):
+        arrange(h)
     pl.semaphore_wait(barrier, len(partners))
 
     def target_x(q):
@@ -329,7 +330,7 @@
     fetched[3].wait()
     w_pair.start()
     depth = ny // 2
-    work = {0: [lambda: arrange(1)], SPREAD: [spread]}
+    work = {SPREAD: [spread]}
     for slot, step in zip(W_SLOTS, (w_first, w_near_step, w_second, w_third, w_fourth)):
         work.setdefault(slot, []).append(step)
     last = n_chunks - 1 + SKEW * (depth - 1) + LAG
@@ -359,9 +360,12 @@
             if q == n_chunks - 1:
                 activations()
             pair(q)
-        if t == NX - 1 + SKEW * (depth - 1) + LAG + WAIT_X:
-            finish(0)
-    finish(1)
+        q = t - SKEW * (depth - 1) - LAG - WAIT_X
+        if q >= 0 and q % NX == NX - 1:
+            finish(q // NX)
+    for q in range(last + 1 - SKEW * (depth - 1) - LAG - WAIT_X, n_chunks):
+        if q % NX == NX - 1:
+            finish(q // NX)
 
     for copy in value_copies:
         copy.wait_recv()

time: 70.2 us -> 67.1 us (0.956)
  the two profiles are of different devices: /device:TPU:66 before, /device:TPU:1 now
where the time goes in v4:
time: 67.1 us; the launch traced here: 66.9 us
  Pallas kernels  66.3 us (99%)
    pallas_call x1, Pallas kernels, body(): pl.pallas_call(functools.partial(kernel, (ny, nz)), out_shape=shapes, in_...  64.5 us
    pallas_call x1, Pallas kernels, body(): pl.pallas_call(hand_over, out_shape=shapes, in_specs=[vmem] * 4, out_spec...  1.7 us

profile of v4, /device:TPU:1, one launch (start us, length us, event | category | flops | bytes accessed | tf_op | source)
XLA Modules:
  0.0 66.9 jit_solution(3909922018172280172)
XLA Ops:
  0.6 64.5 %shard_map.93 = (f32[40,256]{1,0:T(8,128)}, bf16[30,8,256]{2,1,0:T(8,128)(2,1)}, bf16[30,8,256]{2,1,0:T(8,128)(2,1)}, f32[8,40]{1,0:T(8,128)}) custom-call(bf16[40,3840]{1,0:T(8,128)(2,1)} %tok_in.1, s32[8,40]{1,0:T(8,128)} %bitcast.9, bf16[8,40]{1,0:T(8,128)(2,1)} %bitcast.10, bf16[40,256]{1,0:T(8,128)(2,1)} %w_in.1, bf16[30,8,256]{2,1,0:T(8,128)(2,1)} %bitcast.7, ...), custom_call_target="tpu_custom_call" | custom-call | tf_op jit(solution)/shard_map/pallas_call | solution.py:466
  65.2 1.7 %shard_map.94 = (f32[40,256]{1,0:T(8,128)}, bf16[30,8,256]{2,1,0:T(8,128)(2,1)}, bf16[30,8,256]{2,1,0:T(8,128)(2,1)}, f32[8,40]{1,0:T(8,128)}) custom-call(f32[40,256]{1,0:T(8,128)} %get-tuple-element.12.a, bf16[30,8,256]{2,1,0:T(8,128)(2,1)} %get-tuple-element.13.b, bf16[30,8,256]{2,1,0:T(8,128)(2,1)} %get-tuple-element.14.c, f32[8,40]{1,0:T(8,128)} %get-tuple-element.15.d), custom_call_target="tpu_custom_call" | custom-call | tf_op jit(solution)/shard_map/pallas_call | solution.py:479
